TPU v7x, 256 devices: a whole 4x4x8 slice. The times are simulated.
256 devices in a mesh: dp: 4 (over z_lo), space: 8 (over x, z_hi), tensor: 8 (over y, core).
Axes of the slice: x: 4, y: 4, z: 8 (z_hi: 2, z_lo: 4; z = z_hi * 4 + z_lo), core: 2. Of those that a mesh axis runs over, the one named last changes fastest.
Arguments:
- features: bfloat16 [4, 128, 64, 1024], P('dp', ('space', 'tensor')), may hold values from -6 to 6
- kernel: bfloat16 [3, 3, 1024, 1024], P(None, None, 'tensor'), may hold values from -0.0625 to 0.0625
- embedding: float32 [1000, 1024], P(None, 'tensor'), may hold values from -6 to 6
- labels: int32 [4], P('dp'), may hold values from 0 to 999
Outputs:
- weight_grad: float32 [3, 3, 1024, 1024], P(None, None, 'tensor')
- embed_grad: float32 [1000, 1024], P(None, 'tensor')
All inputs are finite; a program needn't handle non-finite values.
Results may differ from a plain program's by a relative error of at most 0.00033.
Values may be sent and summed in bfloat16 or wider, within the bound.
No kernel may reach another device: no remote copies, remote signals or barrier semaphores. Data moves between devices by JAX's collectives and lax.ppermute only.
A program may use at most 64 MiB of HBM per device.

v0:
```python
import math
import jax
import jax.numpy as jnp
from jax import lax
from jax.sharding import PartitionSpec as P

r1_factor = 1000.0


def padded_2(block, sides, width):
    for axis, dim in sides:
        count = lax.axis_size(axis)
        forward = [(i, i + 1) for i in range(count - 1)]
        backward = [(target, source) for source, target in forward]
        low = lax.ppermute(
            lax.slice_in_dim(block, block.shape[dim] - width, None, axis=dim), axis, forward
        )
        high = lax.ppermute(lax.slice_in_dim(block, 0, width, axis=dim), axis, backward)
        block = jnp.concatenate([low, block, high], axis=dim)
    return block


def conv_valid(padded, kern):
    return lax.conv_general_dilated(
        padded,
        kern,
        (1, 1),
        "VALID",
        dimension_numbers=("NHWC", "HWIO", "NHWC"),
        preferred_element_type=jnp.float32,
    )


def pad_cols(field):
    return jnp.pad(field, ((0, 0), (0, 0), (1, 1), (0, 0)))


def taps_of(padded, grad):
    row_count = grad.shape[1]
    col_count = grad.shape[2]
    flat_grad = grad.reshape(-1, grad.shape[3])
    outer = []
    for tap_row in range(3):
        inner = []
        for tap_col in range(3):
            window = padded[
                :, tap_row : tap_row + row_count, tap_col : tap_col + col_count, :
            ].reshape(-1, padded.shape[3])
            inner.append(
                lax.dot_general(
                    window, flat_grad, (((0,), (0,)), ((), ())), preferred_element_type=jnp.float32
                )
            )
        outer.append(jnp.stack(inner))
    return jnp.stack(outer)


def forward_conv(padded, kernel_cols):
    whole = lax.all_gather(padded, "tensor", axis=3, tiled=True)
    return conv_valid(whole, kernel_cols)


def body(features, kernel, embedding, labels):
    tensor_count = lax.axis_size("tensor")
    space_count = lax.axis_size("space")
    image_total = features.shape[0] * lax.axis_size("dp")
    col_count = features.shape[2]
    chan_total = features.shape[3]
    height = features.shape[1] * tensor_count * space_count
    scale = 1.0 / math.sqrt(height * col_count * chan_total)
    gweight = r1_factor / image_total
    local_maps = lax.all_to_all(features, "tensor", split_axis=3, concat_axis=1, tiled=True)
    x_pad = pad_cols(padded_2(local_maps, (("space", 1),), 1))
    kernel_cols = lax.all_to_all(kernel, "tensor", split_axis=3, concat_axis=2, tiled=True)
    hidden = forward_conv(x_pad, kernel_cols)
    class_count = embedding.shape[0]
    onehot = (labels[:, None] == jnp.arange(class_count, dtype=jnp.int32)[None, :]).astype(
        jnp.float32
    )
    embed_rows = jnp.dot(onehot, embedding, precision=lax.Precision.HIGHEST)
    embed_four = embed_rows[:, None, None, :]
    sig = jax.nn.sigmoid(hidden)
    act = hidden * sig
    slope = sig * (1.0 + hidden * (1.0 - sig))
    curve = sig * (1.0 - sig) * (2.0 + hidden * (1.0 - 2.0 * sig))
    score = lax.psum(scale * jnp.sum(act * embed_four, axis=(1, 2, 3)), ("space", "tensor"))
    coeff = -jax.nn.sigmoid(-score) / image_total
    grad_hidden = (embed_four * slope * scale).astype(jnp.bfloat16)
    gh_pad = pad_cols(padded_2(grad_hidden, (("space", 1),), 1))
    flipped = jnp.transpose(kernel[::-1, ::-1], (0, 1, 3, 2))
    gh_whole = lax.all_gather(gh_pad, "tensor", axis=3, tiled=True)
    grad_input = conv_valid(gh_whole, flipped).astype(jnp.bfloat16)
    gx_pad = pad_cols(padded_2(grad_input, (("space", 1),), 1))
    direct = taps_of(gx_pad, gh_whole[:, 1:-1, 1:-1, :])
    second = forward_conv(gx_pad, kernel_cols)
    pre = (
        coeff[:, None, None, None] * embed_four * slope * scale
        + gweight * second * embed_four * curve * scale
    ).astype(jnp.bfloat16)
    adversarial = taps_of(x_pad, lax.all_gather(pre, "tensor", axis=3, tiled=True))
    wgrad = adversarial + gweight * direct
    per_image = coeff[:, None] * scale * jnp.sum(act, axis=(1, 2)) + gweight * scale * jnp.sum(
        second * slope, axis=(1, 2)
    )
    egrad = jnp.dot(onehot.T, per_image, precision=lax.Precision.HIGHEST)
    wtotal, etotal = lax.psum((wgrad, egrad), ("dp", "space"))
    return (wtotal, etotal)


def solution(mesh):
    placed = (
        P("dp", ("space", "tensor"), None, None),
        P(None, None, "tensor", None),
        P(None, "tensor"),
        P("dp"),
    )
    return jax.shard_map(
        body,
        mesh=mesh,
        in_specs=placed,
        out_specs=(P(None, None, "tensor", None), P(None, "tensor")),
        check_vma=False,
    )
```

profile of v0, /device:TPU:1, one launch (start us, length us, event | category | flops | bytes accessed | tf_op | source)
XLA Modules:
  0.0 670.4 jit_solution(11944661111741566787)
XLA Ops:
  7.2 2.1 copy.31
  9.3 1.4 reshape.249
  10.8 12.3 %all_to_all.36 = bf16[8,2,8192]{2,1,0:T(2,128)(2,1)S(1)} all-to-all(bf16[8,2,8192]{2,1,0:T(2,128)(2,1)S(1)} %reshape.249), channel_id=1, replica_groups=mesh['dp'=4,'space'=8,'tensor'=8] {'tensor'}, dimensions={0} | all-to-all | bytes 524288 | tf_op jit(solution)/shard_map/all_to_all | solution.py:72
  26.8 9.4 %collective-permute-start = (bf16[1,1,64,128]{3,2,1,0:T(8,128)(2,1)S(1)}, bf16[1,1,64,128]{3,2,1,0:T(8,128)(2,1)S(1)}, u32[]{:S(2)}, u32[]{:S(2)}) collective-permute-start(bf16[1,1,64,128]{3,2,1,0:T(8,128)(2,1)S(1)} %get-tuple-element.11), channel_id=1, source_target_pairs={{0,8},{8,16},{16,24},{24,32},{32,40},{40,48},{48,56},{1,9},{9,17},... | collective-permute-start | bytes 49160 | tf_op jit(solution)/shard_map/ppermute | solution.py:15
  37.9 3.6 copy.36
  41.5 6.2 all-to-all-start.1
  48.7 47.4 %all-to-all-done.1 = bf16[3,3,128,1024]{2,1,0,3:T(4,128)(2,1)} async-done(((bf16[3,3,128,1024]{2,1,0,3:T(4,128)(2,1)}), bf16[3,3,128,1024]{2,1,0,3:T(4,128)(2,1)}, u32[]{:S(2)}, u32[]{:S(2)}) %all-to-all-start.1) | async-done | bytes 2359328 | tf_op jit(solution)/shard_map/all_to_all | solution.py:74
  96.1 5.6 copy.37
  101.7 3.2 copy.60
  105.5 1.5 copy.35
  107.2 6.5 multiply_convert_fusion
  115.1 9.5 %collective-permute-start.2 = (bf16[1,1,64,128]{3,2,1,0:T(8,128)(2,1)S(1)}, bf16[1,1,64,128]{3,2,1,0:T(8,128)(2,1)S(1)}, u32[]{:S(2)}, u32[]{:S(2)}) collective-permute-start(bf16[1,1,64,128]{3,2,1,0:T(8,128)(2,1)S(1)} %slice.123), channel_id=1, source_target_pairs={{0,8},{8,16},{16,24},{24,32},{32,40},{40,48},{48,56},{1,9},{9,17},... | collective-permute-start | bytes 49160 | tf_op jit(solution)/shard_map/ppermute | solution.py:15
  126.0 39.5 %all-gather.8.cloned.1.call-done = bf16[1,18,66,1024]{3,2,1,0:T(8,128)(2,1)} async-done(((bf16[1,18,66,128]{3,2,1,0:T(8,128)(2,1)}), bf16[1,18,66,1024]{3,2,1,0:T(8,128)(2,1)}) %all-gather.8.cloned.1.call-update) | async-done | bytes 2433040 | tf_op jit(solution)/shard_map/all_gather | solution.py:91
  165.5 3.2 copy.61
  169.2 1.5 copy.44
  170.8 5.7 fusion.81
  178.0 8.0 %collective-permute-start.4 = (bf16[1,1,64,128]{3,2,1,0:T(8,128)(2,1)S(1)}, bf16[1,1,64,128]{3,2,1,0:T(8,128)(2,1)S(1)}, u32[]{:S(2)}, u32[]{:S(2)}) collective-permute-start(bf16[1,1,64,128]{3,2,1,0:T(8,128)(2,1)S(1)} %slice.129), channel_id=1, source_target_pairs={{0,8},{8,16},{16,24},{24,32},{32,40},{40,48},{48,56},{1,9},{9,17},... | collective-permute-start | bytes 49160 | tf_op jit(solution)/shard_map/ppermute | solution.py:15
  188.0 36.1 %all-gather.10.cloned.1.call-done = bf16[1,18,66,1024]{3,2,1,0:T(8,128)(2,1)} async-done(((bf16[1,18,66,128]{3,2,1,0:T(8,128)(2,1)}), bf16[1,18,66,1024]{3,2,1,0:T(8,128)(2,1)}) %all-gather.10.cloned.1.call-update) | async-done | bytes 2433040 | tf_op jit(solution)/shard_map/all_gather | solution.py:59
  224.0 3.2 copy.62
  227.8 1.5 copy.51
  229.6 7.2 %select_reduce_fusion.2 = (f32[128]{0:T(128)S(1)}, f32[128]{0:T(128)S(1)}, f32[]{:T(128)}, f32[16,8,9,128]{3,1,2,0:T(8,128)}) fusion(pred[8,9]{0,1:T(8,128)(4,1)S(1)} %copy-done.17, f32[16,8,9,128]{3,1,2,0:T(8,128)S(1)} %copy-done.15, f32[128]{0:T(128)S(1)} %convolution_bitcast_fusion.9, bf16[3,3,1024,128]{3,2,1,0:T(8,128)(2,1)S(1)} %bitcast.242, ...), kind=kOutput, calls=%fused_computation.90 | convolution fusion | flops 2730147840 | bytes 6710860 | tf_op jit(solution)/shard_map/conv_general_dilated | solution.py:24
  237.5 201.6 %psum.21 = f32[1]{0:T(128)} all-reduce(f32[1]{0:T(128)} %bitcast.13), channel_id=1, replica_groups=mesh['dp'=4,'space'=8,'tensor'=8] {'space','tensor'}, use_global_device_ids=true, to_apply=%region_1.2 | all-reduce | flops 1 | bytes 8 | tf_op jit(solution)/shard_map/psum | solution.py:86
  439.8 1.7 fusion.91
  442.6 1.8 convolution_bitcast_fusion.4
  444.4 1.8 convolution_bitcast_fusion.1
  448.1 1.6 copy-done.7
  453.7 1.9 maximum_bitcast_fusion.3
  456.6 16.8 %all-gather.12.cloned.1.call-done = bf16[16,1,64,1024]{3,2,0,1:T(8,128)(2,1)} async-done(((bf16[16,1,64,128]{3,2,0,1:T(8,128)(2,1)}), bf16[16,1,64,1024]{3,2,0,1:T(8,128)(2,1)}) %all-gather.12.cloned.1.call-update) | async-done | bytes 2097168 | tf_op jit(solution)/shard_map/all_gather | solution.py:100
  473.4 2.2 fusion.69
  481.6 2.7 maximum_add_fusion
  484.3 173.2 %all-reduce.6.cloned.1.call-done = (f32[3,3,128,1024]{3,2,1,0:T(8,128)}, f32[1000,128]{1,0:T(8,128)}) async-done(((f32[3,3,128,1024]{3,2,1,0:T(8,128)}, f32[1000,128]{1,0:T(8,128)}), (f32[3,3,128,1024]{3,2,1,0:T(8,128)}, f32[1000,128]{1,0:T(8,128)})) %all-reduce.6.cloned.1.call-update) | async-done | bytes 5230608 | tf_op jit(solution)/shard_map/psum | solution.py:106
  657.5 5.3 copy.74
  (116 shorter events, 28.6 us)
Async XLA Ops:
  7.2 41.3 %copy-start = (f32[1000,128]{1,0:T(8,128)S(1)}, f32[1000,128]{1,0:T(8,128)}, u32[]{:S(2)}) copy-start(f32[1000,128]{1,0:T(8,128)} %param.6) | copy-start | bytes 1536004
  7.2 30.7 %copy-start.8 = (bf16[3,3,128,1024]{3,2,1,0:T(8,128)(2,1)S(1)}, bf16[3,3,128,1024]{3,2,1,0:T(8,128)(2,1)}, u32[]{:S(2)}) copy-start(bf16[3,3,128,1024]{3,2,1,0:T(8,128)(2,1)} %param.5) | copy-start | bytes 7077892
  7.2 94.5 %all-gather.6.cloned.1.call-start = ((), (), s32[]{:S(2)}) async-start(), calls=%async_computation.2 | async-start | bytes 2985984 | tf_op jit(solution)/shard_map/all_gather | solution.py:59
  25.5 10.8 %collective-permute-start.1 = (bf16[1,1,64,128]{3,2,1,0:T(8,128)(2,1)S(1)}, bf16[1,1,64,128]{3,2,1,0:T(8,128)(2,1)S(1)}, u32[]{:S(2)}, u32[]{:S(2)}) collective-permute-start(bf16[1,1,64,128]{3,2,1,0:T(8,128)(2,1)S(1)} %get-tuple-element.12), channel_id=1, source_target_pairs={{8,0},{16,8},{24,16},{32,24},{40,32},{48,40},{56,48},{9,1},{17,9},... | collective-permute-start | bytes 49160 | tf_op jit(solution)/shard_map/ppermute | solution.py:18
  26.8 10.3 %collective-permute-start = (bf16[1,1,64,128]{3,2,1,0:T(8,128)(2,1)S(1)}, bf16[1,1,64,128]{3,2,1,0:T(8,128)(2,1)S(1)}, u32[]{:S(2)}, u32[]{:S(2)}) collective-permute-start(bf16[1,1,64,128]{3,2,1,0:T(8,128)(2,1)S(1)} %get-tuple-element.11), channel_id=1, source_target_pairs={{0,8},{8,16},{16,24},{24,32},{32,40},{40,48},{48,56},{1,9},{9,17},... | collective-permute-start | bytes 49160 | tf_op jit(solution)/shard_map/ppermute | solution.py:15
  41.5 54.6 %all-to-all-start.1 = ((bf16[3,3,128,1024]{2,1,0,3:T(4,128)(2,1)}), bf16[3,3,128,1024]{2,1,0,3:T(4,128)(2,1)}, u32[]{:S(2)}, u32[]{:S(2)}) async-start(bf16[3,3,128,1024]{2,1,0,3:T(4,128)(2,1)} %copy.36), calls=%async_computation.1 | async-start | bytes 6291456 | tf_op jit(solution)/shard_map/all_to_all | solution.py:74
  47.8 117.7 %all-gather.8.cloned.1.call-start = ((), (), s32[]{:S(2)}) async-start(), calls=%async_computation.3 | async-start | bytes 2985984 | tf_op jit(solution)/shard_map/all_gather | solution.py:91
  105.5 1.7 copy-start.9
  105.5 1.7 copy-start.17
  113.8 11.1 %collective-permute-start.3 = (bf16[1,1,64,128]{3,2,1,0:T(8,128)(2,1)S(1)}, bf16[1,1,64,128]{3,2,1,0:T(8,128)(2,1)S(1)}, u32[]{:S(2)}, u32[]{:S(2)}) collective-permute-start(bf16[1,1,64,128]{3,2,1,0:T(8,128)(2,1)S(1)} %slice.126), channel_id=1, source_target_pairs={{8,0},{16,8},{24,16},{32,24},{40,32},{48,40},{56,48},{9,1},{17,9},... | collective-permute-start | bytes 49160 | tf_op jit(solution)/shard_map/ppermute | solution.py:18
  115.1 9.9 %collective-permute-start.2 = (bf16[1,1,64,128]{3,2,1,0:T(8,128)(2,1)S(1)}, bf16[1,1,64,128]{3,2,1,0:T(8,128)(2,1)S(1)}, u32[]{:S(2)}, u32[]{:S(2)}) collective-permute-start(bf16[1,1,64,128]{3,2,1,0:T(8,128)(2,1)S(1)} %slice.123), channel_id=1, source_target_pairs={{0,8},{8,16},{16,24},{24,32},{32,40},{40,48},{48,56},{1,9},{9,17},... | collective-permute-start | bytes 49160 | tf_op jit(solution)/shard_map/ppermute | solution.py:15
  125.9 98.1 %all-gather.10.cloned.1.call-start = ((), (), s32[]{:S(2)}) async-start(), calls=%async_computation.4 | async-start | bytes 2985984 | tf_op jit(solution)/shard_map/all_gather | solution.py:59
  176.6 10.2 %collective-permute-start.5 = (bf16[1,1,64,128]{3,2,1,0:T(8,128)(2,1)S(1)}, bf16[1,1,64,128]{3,2,1,0:T(8,128)(2,1)S(1)}, u32[]{:S(2)}, u32[]{:S(2)}) collective-permute-start(bf16[1,1,64,128]{3,2,1,0:T(8,128)(2,1)S(1)} %slice.132), channel_id=1, source_target_pairs={{8,0},{16,8},{24,16},{32,24},{40,32},{48,40},{56,48},{9,1},{17,9},... | collective-permute-start | bytes 49160 | tf_op jit(solution)/shard_map/ppermute | solution.py:18
  178.0 8.9 %collective-permute-start.4 = (bf16[1,1,64,128]{3,2,1,0:T(8,128)(2,1)S(1)}, bf16[1,1,64,128]{3,2,1,0:T(8,128)(2,1)S(1)}, u32[]{:S(2)}, u32[]{:S(2)}) collective-permute-start(bf16[1,1,64,128]{3,2,1,0:T(8,128)(2,1)S(1)} %slice.129), channel_id=1, source_target_pairs={{0,8},{8,16},{16,24},{24,32},{32,40},{40,48},{48,56},{1,9},{9,17},... | collective-permute-start | bytes 49160 | tf_op jit(solution)/shard_map/ppermute | solution.py:15
  186.0 0.7 copy-start.14
  186.8 40.4 %copy-start.12 = (bf16[16,1,64,128]{3,2,0,1:T(8,128)(2,1)}, bf16[16,1,64,128]{3,2,0,1:T(8,128)(2,1)S(1)}, u32[]{:S(2)}) copy-start(bf16[16,1,64,128]{3,2,0,1:T(8,128)(2,1)S(1)} %copy.70) | copy-start | bytes 786436
  187.7 285.7 %all-gather.12.cloned.1.call-start = ((), (), s32[]{:S(2)}) async-start(), calls=%async_computation.5 | async-start | bytes 2359296 | tf_op jit(solution)/shard_map/all_gather | solution.py:100
  227.8 1.7 copy-start.10
  227.8 1.8 copy-start.15
  236.8 205.8 %copy-start.6 = (bf16[1,18,66,1024]{3,2,1,0:T(8,128)(2,1)S(1)}, bf16[1,18,66,1024]{3,2,1,0:T(8,128)(2,1)}, u32[]{:S(2)}) copy-start(bf16[1,18,66,1024]{3,2,1,0:T(8,128)(2,1)} %all-gather.8.cloned.1.call-done) | copy-start | bytes 7299076
  442.4 215.2 %all-reduce.6.cloned.1.call-start = ((), (), s32[]{:S(2)}) async-start(), calls=%async_computation.6 | async-start | bytes 10461184 | tf_op jit(solution)/shard_map/psum | solution.py:106
  444.4 1.8 copy-start.11
  447.9 1.8 copy-start.7
  447.9 1.7 copy-start.13
  453.7 19.7 %copy-start.3 = (bf16[1,18,66,128]{3,2,1,0:T(8,128)(2,1)S(1)}, bf16[1,18,66,128]{3,2,1,0:T(8,128)(2,1)}, u32[]{:S(2)}) copy-start(bf16[1,18,66,128]{3,2,1,0:T(8,128)(2,1)} %select_maximum_fusion.4) | copy-start | bytes 912388
  473.4 2.2 copy-start.2
  479.7 1.4 copy-start.4
  479.7 1.9 copy-start.5
  657.5 5.3 copy-start.16
  657.5 6.1 copy-start.1
Sparse Core Ops, SparseCore 0:
  38.0 50.9 all-gather.5
  126.0 39.3 all-gather.7
  187.8 36.1 all-gather.9
  442.5 30.9 all-gather.11
  484.4 173.0 all-reduce.5
where the time goes:
time: 679 us; the launch traced here: 670 us
  waiting for transfers between devices  314 us (46%)
  blocking collectives  214 us (32%)
  local copies, waits for them, and re-layouts  42.6 us (6%)
  starting transfers between devices  37.6 us (6%)
  matrix products  35 us (5%)
  between operations  16.7 us (2%)
  other arithmetic  10.4 us (2%)
    psum x1, blocking collectives, body(): lax.psum(scale * jnp.sum(act * embed_four, axis=(1, 2, 3)), ('space', 'te...  202 us
    psum x1, waiting for transfers between devices, body(): wtotal, etotal = lax.psum((wgrad, egrad), ('dp', 'space'))  173 us
    all_to_all x1, waiting for transfers between devices, body(): lax.all_to_all(kernel, 'tensor', split_axis=3, concat_axis=2, tiled=True)  47.4 us
    all_gather x1, waiting for transfers between devices, body(): gh_whole = lax.all_gather(gh_pad, 'tensor', axis=3, tiled=True)  39.5 us
    all_gather x2, waiting for transfers between devices, forward_conv(): whole = lax.all_gather(padded, 'tensor', axis=3, tiled=True)  36.1 us
    unnamed x48, local copies, waits for them, and re-layouts  28.9 us
    ppermute x3, starting transfers between devices, padded_2(): lax.ppermute(lax.slice_in_dim(block, block.shape[dim] - width, None, axis...  27 us
    conv_general_dilated x3, matrix products, conv_valid(): lax.conv_general_dilated(padded, kern, (1, 1), 'VALID', dimension_numbers...  19.5 us
  transfers between devices with their start and end apart: 12, of which 7 were waited for; matrix products, arithmetic and copies ran while one was open for 3% of the time, Pallas kernels for 0%

commit v1 on v0

--- a/solution.py
+++ b/solution.py
@@ -5,6 +5,10 @@
 from jax.sharding import PartitionSpec as P
 
 r1_factor = 1000.0
+
+
+def _supply_all_record(here_x, axis_key, group_axis):
+    return lax.psum(lax.psum(here_x, axis_key), axis_name=group_axis)
 
 
 def padded_2(block, sides, width):
@@ -83,7 +87,7 @@
     act = hidden * sig
     slope = sig * (1.0 + hidden * (1.0 - sig))
     curve = sig * (1.0 - sig) * (2.0 + hidden * (1.0 - 2.0 * sig))
-    score = lax.psum(scale * jnp.sum(act * embed_four, axis=(1, 2, 3)), ("space", "tensor"))
+    score = _supply_all_record(scale * jnp.sum(act * embed_four, axis=(1, 2, 3)), "space", "tensor")
     coeff = -jax.nn.sigmoid(-score) / image_total
     grad_hidden = (embed_four * slope * scale).astype(jnp.bfloat16)
     gh_pad = pad_cols(padded_2(grad_hidden, (("space", 1),), 1))

time: 679 us -> 515 us (0.76)
  blocking collectives: 214 us -> 57.9 us
  waiting for transfers between devices: 314 us -> 305 us
    psum x1 -> x2, blocking collectives: 202 us -> 45.7 us  [_supply_all_record(): return lax.psum(lax.psum(here_x, axis_key), axis_name=group_axis)]
    all_gather x1, waiting for transfers between devices: 16.8 us -> 7.63 us  [body(): lax.all_gather(pre, 'tensor', axis=3, tiled=True)]
  transfers between devices with their start and end apart: 12 -> 12, of which waited for: 7 -> 7; matrix products, arithmetic and copies ran while one was open for 3% -> 4% of each run, Pallas kernels for 0% -> 0%
where the time goes in v1:
time: 515 us; the launch traced here: 506 us
  waiting for transfers between devices  305 us (59%)
  blocking collectives  57.9 us (11%)
  local copies, waits for them, and re-layouts  42.6 us (8%)
  starting transfers between devices  37.6 us (7%)
  matrix products  35.1 us (7%)
  between operations  16.9 us (3%)
  other arithmetic  10.4 us (2%)
    psum x1, waiting for transfers between devices, body(): wtotal, etotal = lax.psum((wgrad, egrad), ('dp', 'space'))  173 us
    all_to_all x1, waiting for transfers between devices, body(): lax.all_to_all(kernel, 'tensor', split_axis=3, concat_axis=2, tiled=True)  47.4 us
    psum x2, blocking collectives, _supply_all_record(): return lax.psum(lax.psum(here_x, axis_key), axis_name=group_axis)  45.7 us
    all_gather x1, waiting for transfers between devices, body(): gh_whole = lax.all_gather(gh_pad, 'tensor', axis=3, tiled=True)  39.5 us
    all_gather x2, waiting for transfers between devices, forward_conv(): whole = lax.all_gather(padded, 'tensor', axis=3, tiled=True)  36.1 us
    unnamed x48, local copies, waits for them, and re-layouts  28.9 us
    ppermute x3, starting transfers between devices, padded_2(): lax.ppermute(lax.slice_in_dim(block, block.shape[dim] - width, None, axis...  27 us
    conv_general_dilated x3, matrix products, conv_valid(): lax.conv_general_dilated(padded, kern, (1, 1), 'VALID', dimension_numbers...  19.5 us
  transfers between devices with their start and end apart: 12, of which 7 were waited for; matrix products, arithmetic and copies ran while one was open for 4% of the time, Pallas kernels for 0%

profile of v1, /device:TPU:1, one launch (start us, length us, event | category | flops | bytes accessed | tf_op | source)
XLA Modules:
  0.0 505.6 jit_solution(9089792489574850799)
XLA Ops:
  7.2 2.1 copy.31
  10.8 12.3 %all_to_all.36 = bf16[8,2,8192]{2,1,0:T(2,128)(2,1)S(1)} all-to-all(bf16[8,2,8192]{2,1,0:T(2,128)(2,1)S(1)} %reshape.249), channel_id=1, replica_groups=mesh['dp'=4,'space'=8,'tensor'=8] {'tensor'}, dimensions={0} | all-to-all | bytes 524288 | tf_op jit(solution)/shard_map/all_to_all | solution.py:76
  26.8 9.4 %collective-permute-start = (bf16[1,1,64,128]{3,2,1,0:T(8,128)(2,1)S(1)}, bf16[1,1,64,128]{3,2,1,0:T(8,128)(2,1)S(1)}, u32[]{:S(2)}, u32[]{:S(2)}) collective-permute-start(bf16[1,1,64,128]{3,2,1,0:T(8,128)(2,1)S(1)} %get-tuple-element.11), channel_id=1, source_target_pairs={{0,8},{8,16},{16,24},{24,32},{32,40},{40,48},{48,56},{1,9},{9,17},... | collective-permute-start | bytes 49160 | tf_op jit(solution)/shard_map/ppermute | solution.py:19
  37.9 3.6 copy.36
  41.5 6.2 %all-to-all-start.1 = ((bf16[3,3,128,1024]{2,1,0,3:T(4,128)(2,1)}), bf16[3,3,128,1024]{2,1,0,3:T(4,128)(2,1)}, u32[]{:S(2)}, u32[]{:S(2)}) async-start(bf16[3,3,128,1024]{2,1,0,3:T(4,128)(2,1)} %copy.36), calls=%async_computation.1 | async-start | bytes 6291456 | tf_op jit(solution)/shard_map/all_to_all | solution.py:78
  48.7 47.4 %all-to-all-done.1 = bf16[3,3,128,1024]{2,1,0,3:T(4,128)(2,1)} async-done(((bf16[3,3,128,1024]{2,1,0,3:T(4,128)(2,1)}), bf16[3,3,128,1024]{2,1,0,3:T(4,128)(2,1)}, u32[]{:S(2)}, u32[]{:S(2)}) %all-to-all-start.1) | async-done | bytes 2359328 | tf_op jit(solution)/shard_map/all_to_all | solution.py:78
  96.1 5.6 %copy.37 = bf16[3,3,128,8,128]{4,2,3,1,0:T(8,128)(2,1)} copy(bf16[3,3,128,8,128]{2,1,0,4,3:T(4,128)(2,1)} %bitcast.8) | data formatting | bytes 4718592 | tf_op jit(solution)/shard_map/all_to_all | solution.py:78
  101.7 3.2 copy.60
  105.5 1.5 copy.35
  107.2 6.5 %multiply_convert_fusion = (bf16[16,8,9,128]{3,1,2,0:T(8,128)(2,1)S(1)}, f32[16,8,9,128]{3,1,2,0:T(8,128)}) fusion(f32[128]{0:T(128)S(1)} %convolution_bitcast_fusion.9, bf16[3,3,1024,128]{3,2,1,0:T(8,128)(2,1)S(1)} %bitcast.241, bf16[18,1,7,2,1024]{4,2,3,0,1:T(8,128)(2,1)S(1)} %slice.121, bf16[18,1,8,9,1024]{4,2,3,0,1:T(8,128)(2,1)S(1)} %copy.35, ...), kind=kOutput, calls=%fused_computation.88 | convolution fusion | flops 2729263104 | bytes 6414920 | tf_op jit(solution)/shard_map/conv_general_dilated | solution.py:28
  115.1 9.5 %collective-permute-start.2 = (bf16[1,1,64,128]{3,2,1,0:T(8,128)(2,1)S(1)}, bf16[1,1,64,128]{3,2,1,0:T(8,128)(2,1)S(1)}, u32[]{:S(2)}, u32[]{:S(2)}) collective-permute-start(bf16[1,1,64,128]{3,2,1,0:T(8,128)(2,1)S(1)} %slice.123), channel_id=1, source_target_pairs={{0,8},{8,16},{16,24},{24,32},{32,40},{40,48},{48,56},{1,9},{9,17},... | collective-permute-start | bytes 49160 | tf_op jit(solution)/shard_map/ppermute | solution.py:19
  125.9 39.5 %all-gather.8.cloned.1.call-done = bf16[1,18,66,1024]{3,2,1,0:T(8,128)(2,1)} async-done(((bf16[1,18,66,128]{3,2,1,0:T(8,128)(2,1)}), bf16[1,18,66,1024]{3,2,1,0:T(8,128)(2,1)}) %all-gather.8.cloned.1.call-update) | async-done | bytes 2433040 | tf_op jit(solution)/shard_map/all_gather | solution.py:95
  165.5 3.2 copy.61
  169.2 1.5 copy.44
  170.8 5.7 %fusion.81 = bf16[16,8,9,128]{3,1,2,0:T(8,128)(2,1)S(1)} fusion(bf16[3,3,128,1024]{3,2,1,0:T(8,128)(2,1)S(1)} %copy-done.8, bf16[18,1,7,2,1024]{4,2,3,0,1:T(8,128)(2,1)S(1)} %slice.127, bf16[18,1,8,9,1024]{4,2,3,0,1:T(8,128)(2,1)S(1)} %copy.44, pred[8,9]{0,1:T(8,128)(4,1)S(1)} %copy-done.17), kind=kOutput, calls=%fused_computation.73 | convolution fusion | flops 2727936000 | bytes 5824584 | tf_op jit(solution)/shard_map/conv_general_dilated | solution.py:28
  178.0 8.0 %collective-permute-start.4 = (bf16[1,1,64,128]{3,2,1,0:T(8,128)(2,1)S(1)}, bf16[1,1,64,128]{3,2,1,0:T(8,128)(2,1)S(1)}, u32[]{:S(2)}, u32[]{:S(2)}) collective-permute-start(bf16[1,1,64,128]{3,2,1,0:T(8,128)(2,1)S(1)} %slice.129), channel_id=1, source_target_pairs={{0,8},{8,16},{16,24},{24,32},{32,40},{40,48},{48,56},{1,9},{9,17},... | collective-permute-start | bytes 49160 | tf_op jit(solution)/shard_map/ppermute | solution.py:19
  187.9 36.1 %all-gather.10.cloned.1.call-done = bf16[1,18,66,1024]{3,2,1,0:T(8,128)(2,1)} async-done(((bf16[1,18,66,128]{3,2,1,0:T(8,128)(2,1)}), bf16[1,18,66,1024]{3,2,1,0:T(8,128)(2,1)}) %all-gather.10.cloned.1.call-update) | async-done | bytes 2433040 | tf_op jit(solution)/shard_map/all_gather | solution.py:63
  224.0 3.2 copy.62
  227.8 1.5 copy.51
  229.6 7.3 %select_reduce_fusion.2 = (f32[128]{0:T(128)S(1)}, f32[128]{0:T(128)S(1)}, f32[]{:T(128)}, f32[16,8,9,128]{3,1,2,0:T(8,128)}) fusion(pred[8,9]{0,1:T(8,128)(4,1)S(1)} %copy-done.17, f32[16,8,9,128]{3,1,2,0:T(8,128)S(1)} %copy-done.15, f32[128]{0:T(128)S(1)} %convolution_bitcast_fusion.9, bf16[3,3,1024,128]{3,2,1,0:T(8,128)(2,1)S(1)} %bitcast.242, ...), kind=kOutput, calls=%fused_computation.90 | convolution fusion | flops 2730147840 | bytes 6710860 | tf_op jit(solution)/shard_map/conv_general_dilated | solution.py:28
  237.7 29.3 %psum.28 = f32[1]{0:T(128)} all-reduce(f32[1]{0:T(128)} %bitcast.13), channel_id=1, replica_groups=mesh['dp'=4,'space'=8,'tensor'=8] {'space'}, use_global_device_ids=true, to_apply=%region_1.2 | all-reduce | flops 1 | bytes 8 | tf_op jit(solution)/shard_map/psum | solution.py:11
  267.0 16.4 %psum.29 = f32[1]{0:T(128)} all-reduce(f32[1]{0:T(128)} %psum.28), channel_id=1, replica_groups=mesh['dp'=4,'space'=8,'tensor'=8] {'tensor'}, use_global_device_ids=true, to_apply=%region_2.3 | all-reduce | flops 1 | bytes 8 | tf_op jit(solution)/shard_map/psum | solution.py:11
  284.1 1.7 fusion.91
  286.9 1.8 convolution_bitcast_fusion.4
  288.7 1.8 convolution_bitcast_fusion.1
  292.4 1.6 copy-done.7
  298.0 1.9 maximum_bitcast_fusion.3
  300.9 7.6 %all-gather.12.cloned.1.call-done = bf16[16,1,64,1024]{3,2,0,1:T(8,128)(2,1)} async-done(((bf16[16,1,64,128]{3,2,0,1:T(8,128)(2,1)}), bf16[16,1,64,1024]{3,2,0,1:T(8,128)(2,1)}) %all-gather.12.cloned.1.call-update) | async-done | bytes 2097168 | tf_op jit(solution)/shard_map/all_gather | solution.py:104
  308.6 2.2 fusion.69
  316.7 2.7 maximum_add_fusion
  319.4 173.3 %all-reduce.6.cloned.1.call-done = (f32[3,3,128,1024]{3,2,1,0:T(8,128)}, f32[1000,128]{1,0:T(8,128)}) async-done(((f32[3,3,128,1024]{3,2,1,0:T(8,128)}, f32[1000,128]{1,0:T(8,128)}), (f32[3,3,128,1024]{3,2,1,0:T(8,128)}, f32[1000,128]{1,0:T(8,128)})) %all-reduce.6.cloned.1.call-update) | async-done | bytes 5230608 | tf_op jit(solution)/shard_map/psum | solution.py:110
  492.7 5.3 %copy.74 = f32[3,3,128,1024]{3,2,1,0:T(8,128)} copy(f32[3,3,128,1024]{3,2,1,0:T(8,128)} %get-tuple-element.22) | data formatting | bytes 9437184
  (117 shorter events, 30.0 us)
Async XLA Ops:
  7.2 41.3 %copy-start = (f32[1000,128]{1,0:T(8,128)S(1)}, f32[1000,128]{1,0:T(8,128)}, u32[]{:S(2)}) copy-start(f32[1000,128]{1,0:T(8,128)} %param.6) | copy-start | bytes 1536004
  7.2 30.7 %copy-start.8 = (bf16[3,3,128,1024]{3,2,1,0:T(8,128)(2,1)S(1)}, bf16[3,3,128,1024]{3,2,1,0:T(8,128)(2,1)}, u32[]{:S(2)}) copy-start(bf16[3,3,128,1024]{3,2,1,0:T(8,128)(2,1)} %param.5) | copy-start | bytes 7077892
  7.2 94.5 %all-gather.6.cloned.1.call-start = ((), (), s32[]{:S(2)}) async-start(), calls=%async_computation.2 | async-start | bytes 2985984 | tf_op jit(solution)/shard_map/all_gather | solution.py:63
  25.5 10.8 %collective-permute-start.1 = (bf16[1,1,64,128]{3,2,1,0:T(8,128)(2,1)S(1)}, bf16[1,1,64,128]{3,2,1,0:T(8,128)(2,1)S(1)}, u32[]{:S(2)}, u32[]{:S(2)}) collective-permute-start(bf16[1,1,64,128]{3,2,1,0:T(8,128)(2,1)S(1)} %get-tuple-element.12), channel_id=1, source_target_pairs={{8,0},{16,8},{24,16},{32,24},{40,32},{48,40},{56,48},{9,1},{17,9},... | collective-permute-start | bytes 49160 | tf_op jit(solution)/shard_map/ppermute | solution.py:22
  26.8 10.3 %collective-permute-start = (bf16[1,1,64,128]{3,2,1,0:T(8,128)(2,1)S(1)}, bf16[1,1,64,128]{3,2,1,0:T(8,128)(2,1)S(1)}, u32[]{:S(2)}, u32[]{:S(2)}) collective-permute-start(bf16[1,1,64,128]{3,2,1,0:T(8,128)(2,1)S(1)} %get-tuple-element.11), channel_id=1, source_target_pairs={{0,8},{8,16},{16,24},{24,32},{32,40},{40,48},{48,56},{1,9},{9,17},... | collective-permute-start | bytes 49160 | tf_op jit(solution)/shard_map/ppermute | solution.py:19
  41.5 54.6 %all-to-all-start.1 = ((bf16[3,3,128,1024]{2,1,0,3:T(4,128)(2,1)}), bf16[3,3,128,1024]{2,1,0,3:T(4,128)(2,1)}, u32[]{:S(2)}, u32[]{:S(2)}) async-start(bf16[3,3,128,1024]{2,1,0,3:T(4,128)(2,1)} %copy.36), calls=%async_computation.1 | async-start | bytes 6291456 | tf_op jit(solution)/shard_map/all_to_all | solution.py:78
  47.7 117.7 %all-gather.8.cloned.1.call-start = ((), (), s32[]{:S(2)}) async-start(), calls=%async_computation.3 | async-start | bytes 2985984 | tf_op jit(solution)/shard_map/all_gather | solution.py:95
  105.5 1.7 copy-start.9
  105.5 1.7 copy-start.17
  113.8 11.1 %collective-permute-start.3 = (bf16[1,1,64,128]{3,2,1,0:T(8,128)(2,1)S(1)}, bf16[1,1,64,128]{3,2,1,0:T(8,128)(2,1)S(1)}, u32[]{:S(2)}, u32[]{:S(2)}) collective-permute-start(bf16[1,1,64,128]{3,2,1,0:T(8,128)(2,1)S(1)} %slice.126), channel_id=1, source_target_pairs={{8,0},{16,8},{24,16},{32,24},{40,32},{48,40},{56,48},{9,1},{17,9},... | collective-permute-start | bytes 49160 | tf_op jit(solution)/shard_map/ppermute | solution.py:22
  115.1 9.9 %collective-permute-start.2 = (bf16[1,1,64,128]{3,2,1,0:T(8,128)(2,1)S(1)}, bf16[1,1,64,128]{3,2,1,0:T(8,128)(2,1)S(1)}, u32[]{:S(2)}, u32[]{:S(2)}) collective-permute-start(bf16[1,1,64,128]{3,2,1,0:T(8,128)(2,1)S(1)} %slice.123), channel_id=1, source_target_pairs={{0,8},{8,16},{16,24},{24,32},{32,40},{40,48},{48,56},{1,9},{9,17},... | collective-permute-start | bytes 49160 | tf_op jit(solution)/shard_map/ppermute | solution.py:19
  125.9 98.1 %all-gather.10.cloned.1.call-start = ((), (), s32[]{:S(2)}) async-start(), calls=%async_computation.4 | async-start | bytes 2985984 | tf_op jit(solution)/shard_map/all_gather | solution.py:63
  176.6 10.2 %collective-permute-start.5 = (bf16[1,1,64,128]{3,2,1,0:T(8,128)(2,1)S(1)}, bf16[1,1,64,128]{3,2,1,0:T(8,128)(2,1)S(1)}, u32[]{:S(2)}, u32[]{:S(2)}) collective-permute-start(bf16[1,1,64,128]{3,2,1,0:T(8,128)(2,1)S(1)} %slice.132), channel_id=1, source_target_pairs={{8,0},{16,8},{24,16},{32,24},{40,32},{48,40},{56,48},{9,1},{17,9},... | collective-permute-start | bytes 49160 | tf_op jit(solution)/shard_map/ppermute | solution.py:22
  178.0 8.9 %collective-permute-start.4 = (bf16[1,1,64,128]{3,2,1,0:T(8,128)(2,1)S(1)}, bf16[1,1,64,128]{3,2,1,0:T(8,128)(2,1)S(1)}, u32[]{:S(2)}, u32[]{:S(2)}) collective-permute-start(bf16[1,1,64,128]{3,2,1,0:T(8,128)(2,1)S(1)} %slice.129), channel_id=1, source_target_pairs={{0,8},{8,16},{16,24},{24,32},{32,40},{40,48},{48,56},{1,9},{9,17},... | collective-permute-start | bytes 49160 | tf_op jit(solution)/shard_map/ppermute | solution.py:19
  186.0 0.7 copy-start.14
  186.8 40.4 %copy-start.12 = (bf16[16,1,64,128]{3,2,0,1:T(8,128)(2,1)}, bf16[16,1,64,128]{3,2,0,1:T(8,128)(2,1)S(1)}, u32[]{:S(2)}) copy-start(bf16[16,1,64,128]{3,2,0,1:T(8,128)(2,1)S(1)} %copy.70) | copy-start | bytes 786436
  187.7 120.9 %all-gather.12.cloned.1.call-start = ((), (), s32[]{:S(2)}) async-start(), calls=%async_computation.5 | async-start | bytes 2359296 | tf_op jit(solution)/shard_map/all_gather | solution.py:104
  227.8 1.7 copy-start.10
  227.8 1.8 copy-start.15
  236.9 50.0 %copy-start.6 = (bf16[1,18,66,1024]{3,2,1,0:T(8,128)(2,1)S(1)}, bf16[1,18,66,1024]{3,2,1,0:T(8,128)(2,1)}, u32[]{:S(2)}) copy-start(bf16[1,18,66,1024]{3,2,1,0:T(8,128)(2,1)} %all-gather.8.cloned.1.call-done) | copy-start | bytes 7299076
  286.6 206.1 %all-reduce.6.cloned.1.call-start = ((), (), s32[]{:S(2)}) async-start(), calls=%async_computation.6 | async-start | bytes 10461184 | tf_op jit(solution)/shard_map/psum | solution.py:110
  288.7 1.8 copy-start.11
  292.2 1.8 copy-start.7
  292.2 1.7 copy-start.13
  298.0 10.6 %copy-start.3 = (bf16[1,18,66,128]{3,2,1,0:T(8,128)(2,1)S(1)}, bf16[1,18,66,128]{3,2,1,0:T(8,128)(2,1)}, u32[]{:S(2)}) copy-start(bf16[1,18,66,128]{3,2,1,0:T(8,128)(2,1)} %select_maximum_fusion.4) | copy-start | bytes 912388
  308.6 2.2 copy-start.2
  314.8 1.4 copy-start.4
  314.8 1.9 copy-start.5
  492.7 5.3 %copy-start.16 = (f32[1000,128]{1,0:T(8,128)S(1)}, f32[1000,128]{1,0:T(8,128)}, u32[]{:S(2)}) copy-start(f32[1000,128]{1,0:T(8,128)} %get-tuple-element.23) | copy-start | bytes 1536004
  492.7 6.1 %copy-start.1 = (f32[1000,128]{1,0:T(8,128)S(1)}, f32[1000,128]{1,0:T(8,128)}, u32[]{:S(2)}) copy-start(f32[1000,128]{1,0:T(8,128)} %param.6) | copy-start | bytes 1536004
Sparse Core Ops, SparseCore 0:
  38.0 50.9 all-gather.5
  126.0 39.3 all-gather.7
  187.8 36.1 all-gather.9
  286.8 21.7 all-gather.11
  319.5 173.1 all-reduce.5
